TPU v7x, 512 devices: a whole 4x4x16 slice. The times are simulated.
512 devices in a mesh: rep: 16 (over z), ep: 32 (over y, x, core).
Axes of the slice: x: 4, y: 4, z: 16, core: 2. Of those that a mesh axis runs over, the one named last changes fastest.
Arguments:
- tokens: bfloat16 [2048, 4096], P('rep'), may hold values from -6 to 6
- routes: int32 [2048, 2], P('rep'), may hold values from 0 to 7, all different within a row; in each aligned block of 128 rows (0 to 127, 128 to 255, ...) at most 64 rows name the same one
- gates: bfloat16 [2048, 2], P('rep'), may hold values from 0.19921875 to 1
- w_gate: bfloat16 [32, 1792, 4096], P('ep', 'rep'), may hold values from -0.09375 to 0.09375
- w_up: bfloat16 [32, 1792, 4096], P('ep', 'rep'), may hold values from -0.09375 to 0.09375
- direction: bfloat16 [32, 1792, 4096], P('ep', None, 'rep'), may hold values from -32 to 32
Outputs:
- next_direction: bfloat16 [32, 1792, 4096], P('ep', None, 'rep')
- rayleigh: float32 [1], replicated
Inputs may be any that keep to these rules, and one draw needn't show every extreme that they name: `routes`: each row names two different experts. In each aligned block of 128 rows (the tokens of one replica) no expert is named by more than 64 rows, and in some block some expert is named by exactly 64 rows.
All inputs are finite; a program needn't handle non-finite values.
Results may differ from a plain program's by a relative error of at most 0.007.
Values may be sent and summed in bfloat16 or wider, within the bound.
A program may use at most 64 MiB of HBM per device.

v0:
```python
import jax
import jax.numpy as jnp
from jax import lax
from jax.sharding import PartitionSpec as P

D = 4096
FF = 7168
EXPERTS = 8
ITERS = 2
CAP = 64


def own_slots(route_rows, expert, depth):
    pairs = route_rows.reshape(-1)
    hits = (pairs == expert).astype(jnp.int32)
    rank = jnp.cumsum(hits) - hits
    slots = jnp.arange(depth, dtype=jnp.int32)[:, None]
    return ((slots == rank[None, :]) & (hits[None, :] > 0)).astype(jnp.float32)


def on_device(tokens, routes, gates, w_gate, w_up, direction):
    n_rep = lax.axis_size("rep")
    n_ep = lax.axis_size("ep")
    slices = n_ep // EXPERTS
    local = tokens.shape[0]
    depth = CAP
    expert = lax.axis_index("ep") // slices
    route_all = lax.all_gather(routes, "rep", axis=0, tiled=True).reshape(n_rep, local, 2)
    tables = jax.vmap(lambda chosen: own_slots(chosen, expert, depth))(route_all)
    token_map = tables.reshape(n_rep, depth, local, 2).sum(axis=3)
    own_table = lax.dynamic_index_in_dim(tables, lax.axis_index("rep"), 0, keepdims=False)
    own_tokens = own_table.reshape(depth, local, 2).sum(axis=2)
    picked = jnp.dot(
        own_tokens.astype(jnp.bfloat16), tokens, preferred_element_type=jnp.float32
    ).astype(jnp.bfloat16)
    picked_gate = jnp.dot(
        own_table, gates.reshape(-1).astype(jnp.float32), precision=lax.Precision.HIGHEST
    ).astype(jnp.bfloat16)
    rows, rates = (
        lax.all_gather(picked, "rep", axis=0, tiled=True),
        lax.all_gather(picked_gate, "rep", axis=0, tiled=True),
    )
    contract = (((1,), (1,)), ((), ()))
    pre_gate = lax.dot_general(w_gate[0], rows, contract, preferred_element_type=jnp.float32)
    pre_up = lax.dot_general(w_up[0], rows, contract, preferred_element_type=jnp.float32)
    gated = (jax.nn.silu(pre_gate) * pre_up * rates.astype(jnp.float32)[None, :]).astype(
        jnp.bfloat16
    )
    hidden_t = lax.all_gather(gated, "rep", axis=0, tiled=True)
    current = direction[0]
    columns = current.shape[1]
    count = float(EXPERTS * FF * D)
    rayleigh = jnp.zeros((), jnp.float32)
    first_dims = (((0,), (0,)), ((), ()))
    for step in range(ITERS):
        partial_value = lax.dot_general(
            hidden_t, current, first_dims, preferred_element_type=jnp.float32
        ).reshape(n_rep, depth, columns)
        spread = jnp.einsum(
            "rst,rsd->rtd", token_map, partial_value, precision=lax.Precision.HIGHEST
        ).reshape(n_rep * local, columns)
        tangent = lax.psum_scatter(spread, "ep", scatter_dimension=0, tiled=True)
        piece = tangent.astype(jnp.bfloat16)
        sent = lax.all_gather(piece, "ep", axis=0, tiled=True)
        current_f = current.astype(jnp.float32)
        arrived = jnp.einsum(
            "rst,rtd->rsd",
            token_map.astype(jnp.bfloat16),
            sent.reshape(n_rep, local, columns),
            preferred_element_type=jnp.float32,
        ).astype(jnp.bfloat16)
        product = (
            jnp.dot(
                hidden_t,
                arrived.reshape(n_rep * depth, columns),
                preferred_element_type=jnp.float32,
            )
            / n_rep
        )
        energy, cross, square = lax.psum(
            (
                jnp.sum(product * product),
                jnp.sum(current_f * product),
                jnp.sum(current_f * current_f),
            ),
            ("rep", "ep"),
        )
        rayleigh = cross / count / (square / count + 1e-06)
        current = (product * lax.rsqrt(energy / count + 1e-06)).astype(jnp.bfloat16)
    return (current[None], rayleigh.reshape(1))


def solution(mesh):
    return jax.shard_map(
        on_device,
        mesh=mesh,
        in_specs=(
            P("rep", None),
            P("rep", None),
            P("rep", None),
            P("ep", "rep", None),
            P("ep", "rep", None),
            P("ep", None, "rep"),
        ),
        out_specs=(P("ep", None, "rep"), P()),
        check_vma=False,
    )
```

profile of v0, /device:TPU:1, one launch (start us, length us, event | category | flops | bytes accessed | tf_op | source)
XLA Modules:
  0.0 805.5 jit_solution(234640360543273105)
XLA Ops:
  7.2 29.7 %all_gather.18 = s32[2048,2]{0,1:T(2,128)S(1)} all-gather(s32[128,2]{0,1:T(2,128)} %param.7), channel_id=1, replica_groups=mesh['rep'=16,'ep'=32] {'rep'}, dimensions={0}, use_global_device_ids=true | all-gather | bytes 17408 | tf_op jit(solution)/shard_map/all_gather | solution.py:28
  37.0 0.4 copy.50
  37.3 0.6 reshape.108
  38.0 0.5 reshape.109
  38.4 0.6 reduce-window.6
  39.3 1.4 fusion
  41.0 1.1 convolution_convert_fusion
  42.5 1.3 dynamic-slice
  44.7 20.1 %all-reduce = bf16[1024]{0:T(1024)(128)(2,1)S(1)} all-reduce(bf16[1024]{0:T(1024)(128)(2,1)S(1)} %dynamic-update-slice), channel_id=1, replica_groups=mesh['rep'=16,'ep'=32] {'rep'}, use_global_device_ids=true, to_apply=%add | all-reduce | flops 1024 | bytes 4096
  64.8 86.5 %all-gather.5.cloned.1.call-done = bf16[1024,4096]{1,0:T(8,128)(2,1)} async-done(((bf16[64,4096]{1,0:T(8,128)(2,1)}), bf16[1024,4096]{1,0:T(8,128)(2,1)}) %all-gather.5.cloned.1.call-update) | async-done | bytes 8388624 | tf_op jit(solution)/shard_map/all_gather | solution.py:40
  151.3 6.4 convolution_bitcast_fusion.1
  157.7 3.5 fusion.5
  161.8 0.2 convert_reduce_fusion
  162.1 66.3 %all-gather.7.cloned.1.call-done = bf16[1792,1024]{1,0:T(8,128)(2,1)} async-done(((bf16[112,1024]{1,0:T(8,128)(2,1)}), bf16[1792,1024]{1,0:T(8,128)(2,1)}) %all-gather.7.cloned.1.call-update) | async-done | bytes 3670032 | tf_op jit(solution)/shard_map/all_gather | solution.py:49
  228.3 6.0 copy.60
  234.4 3.2 fusion.9
  237.5 3.2 fusion.20
  240.8 105.8 %reduce-scatter.3.cloned.1.call-done = f32[64,256]{1,0:T(8,128)} async-done(((f32[2048,256]{1,0:T(8,128)}), f32[64,256]{1,0:T(8,128)}) %reduce-scatter.3.cloned.1.call-update) | async-done | bytes 65552 | tf_op jit(solution)/shard_map/reduce_scatter | solution.py:62
  346.6 1.5 convert_element_type.87
  348.3 61.5 %all-gather.9.cloned.1.call-done = bf16[2048,256]{1,0:T(8,128)(2,1)} async-done(((bf16[64,256]{1,0:T(8,128)(2,1)}), bf16[2048,256]{1,0:T(8,128)(2,1)}) %all-gather.9.cloned.1.call-update) | async-done | bytes 1048592 | tf_op jit(solution)/shard_map/all_gather | solution.py:64
  409.8 1.5 convolution_convert_fusion.2
  411.3 3.8 multiply_reduce_fusion.1
  415.1 103.6 %psum.28 = f32[]{:T(128)} all-reduce(f32[]{:T(128)} %get-tuple-element.8), channel_id=1, replica_groups=mesh['rep'=16,'ep'=32] {'rep','ep'}, use_global_device_ids=true, to_apply=%region_6.7 | all-reduce | flops 1 | bytes 8 | tf_op jit(solution)/shard_map/psum | solution.py:80
  519.4 3.2 fusion.19
  522.6 3.2 fusion.21
  526.0 95.4 %reduce-scatter.5.cloned.1.call-done = f32[64,256]{1,0:T(8,128)} async-done(((f32[2048,256]{1,0:T(8,128)}), f32[64,256]{1,0:T(8,128)}) %reduce-scatter.5.cloned.1.call-update) | async-done | bytes 65552 | tf_op jit(solution)/shard_map/reduce_scatter | solution.py:62
  621.3 1.5 convert_element_type.90
  622.8 61.7 %all-gather.11.cloned.1.call-done = bf16[2048,256]{1,0:T(8,128)(2,1)} async-done(((bf16[64,256]{1,0:T(8,128)(2,1)}), bf16[2048,256]{1,0:T(8,128)(2,1)}) %all-gather.11.cloned.1.call-update) | async-done | bytes 1048592 | tf_op jit(solution)/shard_map/all_gather | solution.py:64
  684.5 1.5 convolution_convert_fusion.1
  686.1 4.6 fusion.1
  690.6 103.8 %all-reduce.1 = (f32[]{:T(128)}, f32[]{:T(128)}, f32[]{:T(128)}) all-reduce(f32[]{:T(128)} %get-tuple-element.3, f32[]{:T(128)} %get-tuple-element.2, f32[]{:T(128)} %get-tuple-element.4), channel_id=1, replica_groups=mesh['rep'=16,'ep'=32] {'rep','ep'}, use_global_device_ids=true, to_apply=%region_9.10 | all-reduce | flops 3 | bytes 24 | tf_op jit(solution)/shard_map/psum | solution.py:80
  796.5 1.1 fusion.8
  (51 shorter events, 2.1 us)
Async XLA Ops:
  7.2 33.8 %copy-start = (bf16[128,4096]{1,0:T(8,128)(2,1)S(1)}, bf16[128,4096]{1,0:T(8,128)(2,1)}, u32[]{:S(2)}) copy-start(bf16[128,4096]{1,0:T(8,128)(2,1)} %param.6) | copy-start | bytes 3145732
  7.2 144.1 %all-gather.5.cloned.1.call-start = ((), (), s32[]{:S(2)}) async-start(), calls=%async_computation.2 | async-start | bytes 8912896 | tf_op jit(solution)/shard_map/all_gather | solution.py:40
  37.9 4.2 copy-start.1
  38.0 113.3 %copy-start.3 = (bf16[1,112,4096]{2,1,0:T(8,128)(2,1)S(1)}, bf16[1,112,4096]{2,1,0:T(8,128)(2,1)}, u32[]{:S(2)}) copy-start(bf16[1,112,4096]{2,1,0:T(8,128)(2,1)} %param.9) | copy-start | bytes 2752516
  42.1 186.2 %all-gather.7.cloned.1.call-start = ((), (), s32[]{:S(2)}) async-start(), calls=%async_computation.3 | async-start | bytes 3899392 | tf_op jit(solution)/shard_map/all_gather | solution.py:49
  151.3 6.4 copy-start.2
  151.3 6.4 copy-start.4
  161.3 185.3 %reduce-scatter.3.cloned.1.call-start = ((), (), s32[]{:S(2)}) async-start(), calls=%async_computation.4 | async-start | bytes 2162688 | tf_op jit(solution)/shard_map/reduce_scatter | solution.py:62
  228.3 6.0 copy-start.5
  240.8 169.0 %all-gather.9.cloned.1.call-start = ((), (), s32[]{:S(2)}) async-start(), calls=%async_computation.5 | async-start | bytes 1081344 | tf_op jit(solution)/shard_map/all_gather | solution.py:64
  348.1 273.2 %reduce-scatter.5.cloned.1.call-start = ((), (), s32[]{:S(2)}) async-start(), calls=%async_computation.6 | async-start | bytes 2162688 | tf_op jit(solution)/shard_map/reduce_scatter | solution.py:62
  415.1 107.5 %copy-start.6 = (f32[1792,256]{1,0:T(8,128)}, f32[1792,256]{1,0:T(8,128)S(1)}, u32[]{:S(2)}) copy-start(f32[1792,256]{1,0:T(8,128)S(1)} %get-tuple-element.9) | copy-start | bytes 5505028
  525.9 158.6 %all-gather.11.cloned.1.call-start = ((), (), s32[]{:S(2)}) async-start(), calls=%async_computation.7 | async-start | bytes 1081344 | tf_op jit(solution)/shard_map/all_gather | solution.py:64
Sparse Core Ops, SparseCore 0:
  42.2 109.0 all-gather.4
  161.4 66.8 all-gather.6
  240.9 105.6 reduce-scatter.2
  350.2 59.5 all-gather.8
  526.0 95.2 reduce-scatter.4
  624.9 59.5 all-gather.10
where the time goes:
time: 806 us
  waiting for transfers between devices  477 us (59%)
  blocking collectives  257 us (32%)
  matrix products  35.4 us (4%)
  between operations  18.9 us (2%)
  local copies, waits for them, and re-layouts  9.84 us (1%)
    psum x2, blocking collectives, on_device(): lax.psum((jnp.sum(product * product), jnp.sum(current_f * product), jnp.s...  207 us
    reduce_scatter x2, waiting for transfers between devices, on_device(): tangent = lax.psum_scatter(spread, 'ep', scatter_dimension=0, tiled=True)  201 us
    all_gather x2, waiting for transfers between devices, on_device(): sent = lax.all_gather(piece, 'ep', axis=0, tiled=True)  123 us
    all_gather x1, waiting for transfers between devices, on_device(): lax.all_gather(picked, 'rep', axis=0, tiled=True)  86.5 us
    all_gather x1, waiting for transfers between devices, on_device(): hidden_t = lax.all_gather(gated, 'rep', axis=0, tiled=True)  66.3 us
    all_gather x1, blocking collectives, on_device(): lax.all_gather(routes, 'rep', axis=0, tiled=True).reshape(n_rep, local, 2)  29.7 us
    unnamed x1, blocking collectives  20.1 us
  transfers between devices with their start and end apart: 6, of which 6 were waited for; matrix products, arithmetic and copies ran while one was open for 0% of the time, Pallas kernels for 0%

commit v1 on v0

--- a/solution.py
+++ b/solution.py
@@ -8,6 +8,11 @@
 EXPERTS = 8
 ITERS = 2
 CAP = 64
+
+
+def gather_over(array, mesh_axis, along):
+    sent = jnp.stack([array] * lax.axis_size(mesh_axis))
+    return jnp.concatenate(lax.all_to_all(sent, mesh_axis, 0, 0), axis=along)
 
 
 def own_slots(route_rows, expert, depth):
@@ -46,7 +51,7 @@
     gated = (jax.nn.silu(pre_gate) * pre_up * rates.astype(jnp.float32)[None, :]).astype(
         jnp.bfloat16
     )
-    hidden_t = lax.all_gather(gated, "rep", axis=0, tiled=True)
+    hidden_t = gather_over(gated, "rep", 0)
     current = direction[0]
     columns = current.shape[1]
     count = float(EXPERTS * FF * D)

time: 806 us -> 904 us (1.12)
  waiting for transfers between devices: 477 us -> 565 us
    all_to_all x0 -> x1, waiting for transfers between devices: none -> 159 us  [gather_over(): return jnp.concatenate(lax.all_to_all(sent, mesh_axis, 0, 0), axis=along)]
    all_gather x1 -> x0, waiting for transfers between devices: 66.3 us -> none  [on_device(): hidden_t = lax.all_gather(gated, 'rep', axis=0, tiled=True)]
where the time goes in v1:
time: 904 us; the launch traced here: 903 us
  waiting for transfers between devices  565 us (62%)
  blocking collectives  257 us (28%)
  matrix products  34.7 us (4%)
  between operations  18.6 us (2%)
  local copies, waits for them, and re-layouts  12.2 us (1%)
    psum x2, blocking collectives, on_device(): lax.psum((jnp.sum(product * product), jnp.sum(current_f * product), jnp.s...  207 us
    reduce_scatter x2, waiting for transfers between devices, on_device(): tangent = lax.psum_scatter(spread, 'ep', scatter_dimension=0, tiled=True)  196 us
    all_to_all x1, waiting for transfers between devices, gather_over(): return jnp.concatenate(lax.all_to_all(sent, mesh_axis, 0, 0), axis=along)  159 us
    all_gather x2, waiting for transfers between devices, on_device(): sent = lax.all_gather(piece, 'ep', axis=0, tiled=True)  123 us
    all_gather x1, waiting for transfers between devices, on_device(): lax.all_gather(picked, 'rep', axis=0, tiled=True)  86.6 us
    all_gather x1, blocking collectives, on_device(): lax.all_gather(routes, 'rep', axis=0, tiled=True).reshape(n_rep, local, 2)  29.7 us
    unnamed x1, blocking collectives  20.1 us
  transfers between devices with their start and end apart: 6, of which 6 were waited for; matrix products, arithmetic and copies ran while one was open for 0% of the time, Pallas kernels for 0%

profile of v1, /device:TPU:1, one launch (start us, length us, event | category | flops | bytes accessed | tf_op | source)
XLA Modules:
  0.0 902.8 jit_solution(6173712533364615512)
XLA Ops:
  7.2 29.7 %all_gather.15 = s32[2048,2]{0,1:T(2,128)S(1)} all-gather(s32[128,2]{0,1:T(2,128)} %param.7), channel_id=1, replica_groups=mesh['rep'=16,'ep'=32] {'rep'}, dimensions={0}, use_global_device_ids=true | all-gather | bytes 17408 | tf_op jit(solution)/shard_map/all_gather | solution.py:33
  37.3 0.5 reshape.113
  37.8 0.6 reshape.112
  38.5 0.6 reduce-window.6
  39.4 1.4 fusion
  41.0 1.1 convolution_convert_fusion
  42.4 1.3 dynamic-slice
  44.7 20.1 %all-reduce = bf16[1024]{0:T(1024)(128)(2,1)S(1)} all-reduce(bf16[1024]{0:T(1024)(128)(2,1)S(1)} %dynamic-update-slice), channel_id=1, replica_groups=mesh['rep'=16,'ep'=32] {'rep'}, use_global_device_ids=true, to_apply=%add | all-reduce | flops 1024 | bytes 4096
  64.8 86.6 %all-gather.4.cloned.1.call-done = bf16[1024,4096]{1,0:T(8,128)(2,1)} async-done(((bf16[64,4096]{1,0:T(8,128)(2,1)}), bf16[1024,4096]{1,0:T(8,128)(2,1)}) %all-gather.4.cloned.1.call-update) | async-done | bytes 8388624 | tf_op jit(solution)/shard_map/all_gather | solution.py:45
  151.3 6.4 convolution_bitcast_fusion.1
  157.7 2.8 fusion.5
  160.6 2.3 stack.2
  162.9 8.6 all-to-all-start
  172.3 158.5 %all-to-all-done = bf16[16,112,1024]{2,1,0:T(8,128)(2,1)} async-done(((bf16[16,112,1024]{2,1,0:T(8,128)(2,1)}), bf16[16,112,1024]{2,1,0:T(8,128)(2,1)}, u32[]{:S(2)}, u32[]{:S(2)}) %all-to-all-start) | async-done | bytes 3670048 | tf_op jit(solution)/shard_map/all_to_all | solution.py:15
  330.8 6.0 copy.60
  336.8 3.2 fusion.11
  340.0 3.3 fusion.21
  343.4 100.7 %reduce-scatter.3.cloned.1.call-done = f32[64,256]{1,0:T(8,128)} async-done(((f32[2048,256]{1,0:T(8,128)}), f32[64,256]{1,0:T(8,128)}) %reduce-scatter.3.cloned.1.call-update) | async-done | bytes 65552 | tf_op jit(solution)/shard_map/reduce_scatter | solution.py:67
  444.1 1.5 convert_element_type.87
  445.8 61.6 %all-gather.6.cloned.1.call-done = bf16[2048,256]{1,0:T(8,128)(2,1)} async-done(((bf16[64,256]{1,0:T(8,128)(2,1)}), bf16[2048,256]{1,0:T(8,128)(2,1)}) %all-gather.6.cloned.1.call-update) | async-done | bytes 1048592 | tf_op jit(solution)/shard_map/all_gather | solution.py:69
  507.4 1.5 convolution_convert_fusion.2
  508.9 3.8 multiply_reduce_fusion.1
  512.7 103.6 %psum.28 = f32[]{:T(128)} all-reduce(f32[]{:T(128)} %get-tuple-element.8), channel_id=1, replica_groups=mesh['rep'=16,'ep'=32] {'rep','ep'}, use_global_device_ids=true, to_apply=%region_6.7 | all-reduce | flops 1 | bytes 8 | tf_op jit(solution)/shard_map/psum | solution.py:85
  617.0 3.2 fusion.9
  620.2 3.2 fusion.22
  623.5 95.4 %reduce-scatter.5.cloned.1.call-done = f32[64,256]{1,0:T(8,128)} async-done(((f32[2048,256]{1,0:T(8,128)}), f32[64,256]{1,0:T(8,128)}) %reduce-scatter.5.cloned.1.call-update) | async-done | bytes 65552 | tf_op jit(solution)/shard_map/reduce_scatter | solution.py:67
  718.9 1.5 convert_element_type.90
  720.4 61.7 %all-gather.8.cloned.1.call-done = bf16[2048,256]{1,0:T(8,128)(2,1)} async-done(((bf16[64,256]{1,0:T(8,128)(2,1)}), bf16[2048,256]{1,0:T(8,128)(2,1)}) %all-gather.8.cloned.1.call-update) | async-done | bytes 1048592 | tf_op jit(solution)/shard_map/all_gather | solution.py:69
  782.1 1.5 convolution_convert_fusion.1
  783.6 4.6 fusion.1
  788.1 103.8 %all-reduce.1 = (f32[]{:T(128)}, f32[]{:T(128)}, f32[]{:T(128)}) all-reduce(f32[]{:T(128)} %get-tuple-element.3, f32[]{:T(128)} %get-tuple-element.2, f32[]{:T(128)} %get-tuple-element.4), channel_id=1, replica_groups=mesh['rep'=16,'ep'=32] {'rep','ep'}, use_global_device_ids=true, to_apply=%region_9.10 | all-reduce | flops 3 | bytes 24 | tf_op jit(solution)/shard_map/psum | solution.py:85
  894.0 1.1 fusion.8
  (51 shorter events, 2.7 us)
Async XLA Ops:
  7.2 33.8 %copy-start = (bf16[128,4096]{1,0:T(8,128)(2,1)S(1)}, bf16[128,4096]{1,0:T(8,128)(2,1)}, u32[]{:S(2)}) copy-start(bf16[128,4096]{1,0:T(8,128)(2,1)} %param.6) | copy-start | bytes 3145732
  7.2 144.1 %all-gather.4.cloned.1.call-start = ((), (), s32[]{:S(2)}) async-start(), calls=%async_computation.3 | async-start | bytes 8912896 | tf_op jit(solution)/shard_map/all_gather | solution.py:45
  37.8 4.3 copy-start.2
  37.8 113.5 %copy-start.4 = (bf16[1,112,4096]{2,1,0:T(8,128)(2,1)S(1)}, bf16[1,112,4096]{2,1,0:T(8,128)(2,1)}, u32[]{:S(2)}) copy-start(bf16[1,112,4096]{2,1,0:T(8,128)(2,1)} %param.9) | copy-start | bytes 2752516
  151.3 6.4 copy-start.3
  151.3 6.4 copy-start.5
  162.9 167.9 %all-to-all-start = ((bf16[16,112,1024]{2,1,0:T(8,128)(2,1)}), bf16[16,112,1024]{2,1,0:T(8,128)(2,1)}, u32[]{:S(2)}, u32[]{:S(2)}) async-start(bf16[16,112,1024]{2,1,0:T(8,128)(2,1)} %stack.2), calls=%async_computation | async-start | bytes 7340032 | tf_op jit(solution)/shard_map/all_to_all | solution.py:15
  171.5 272.6 %reduce-scatter.3.cloned.1.call-start = ((), (), s32[]{:S(2)}) async-start(), calls=%async_computation.4 | async-start | bytes 2162688 | tf_op jit(solution)/shard_map/reduce_scatter | solution.py:67
  330.8 6.0 copy-start.6
  343.3 164.1 %all-gather.6.cloned.1.call-start = ((), (), s32[]{:S(2)}) async-start(), calls=%async_computation.5 | async-start | bytes 1081344 | tf_op jit(solution)/shard_map/all_gather | solution.py:69
  445.5 273.3 %reduce-scatter.5.cloned.1.call-start = ((), (), s32[]{:S(2)}) async-start(), calls=%async_computation.6 | async-start | bytes 2162688 | tf_op jit(solution)/shard_map/reduce_scatter | solution.py:67
  512.7 107.5 %copy-start.1 = (f32[1792,256]{1,0:T(8,128)}, f32[1792,256]{1,0:T(8,128)S(1)}, u32[]{:S(2)}) copy-start(f32[1792,256]{1,0:T(8,128)S(1)} %get-tuple-element.9) | copy-start | bytes 5505028
  623.5 158.6 %all-gather.8.cloned.1.call-start = ((), (), s32[]{:S(2)}) async-start(), calls=%async_computation.7 | async-start | bytes 1081344 | tf_op jit(solution)/shard_map/all_gather | solution.py:69
Sparse Core Ops, SparseCore 0:
  42.2 109.0 all-gather.3
  343.4 100.5 reduce-scatter.2
  447.8 59.5 all-gather.5
  623.6 95.2 reduce-scatter.4
  722.4 59.5 all-gather.7
